TPU v7x, 128 devices: a whole 4x4x4 slice. The times are simulated.
128 devices in a mesh: seq: 64 (over x, z, y), head: 2 (over core).
Axes of the slice: x: 4, y: 4, z: 4, core: 2. Of those that a mesh axis runs over, the one named last changes fastest.
Arguments:
- layer_input: bfloat16 [2, 8192, 2048], P(None, 'seq', 'head'), may hold values from -6 to 6
- w_q: bfloat16 [2048, 2048], P('seq', 'head'), may hold values from -0.125 to 0.125
- w_f: bfloat16 [2048, 2048], P('seq', 'head'), may hold values from -0.125 to 0.125
- w_i: bfloat16 [2048, 2048], P('seq', 'head'), may hold values from -0.125 to 0.125
- conv_weight: bfloat16 [3, 4, 2048], P(None, None, 'head'), may hold values from -3 to 3
- forget_gap: bfloat16 [2048], P('head'), may hold values from 9.953976e-06 to 0.099609375
- gain_out: bfloat16 [2048], P('head'), may hold values from 0.5 to 1.5
- w_o: bfloat16 [2048, 2048], P('head', 'seq'), may hold values from -0.125 to 0.125
- gain_attn: bfloat16 [2048], P('head'), may hold values from 0.5 to 1.5
- gain_ffn: bfloat16 [2048], P('head'), may hold values from 0.5 to 1.5
- w_gate: bfloat16 [2048, 5632], P('seq', 'head'), may hold values from -0.125 to 0.125
- w_up: bfloat16 [2048, 5632], P('seq', 'head'), may hold values from -0.125 to 0.125
- w_down: bfloat16 [5632, 2048], P('head', 'seq'), may hold values from -0.078125 to 0.078125
- out_grad: bfloat16 [2, 8192, 2048], P(None, 'seq', 'head'), may hold values from -6 to 6
Outputs:
- output: bfloat16 [2, 8192, 2048], P(None, 'seq', 'head')
- input_grad: bfloat16 [2, 8192, 2048], P(None, 'seq', 'head')
- grad_w_q: float32 [2048, 2048], P('seq', 'head')
- grad_w_f: float32 [2048, 2048], P('seq', 'head')
- grad_w_i: float32 [2048, 2048], P('seq', 'head')
- grad_conv: float32 [3, 4, 2048], P(None, None, 'head')
- grad_forget_gap: float32 [2048], P('head')
- grad_gain_out: float32 [2048], P('head')
- grad_w_o: float32 [2048, 2048], P('head', 'seq')
- grad_gain_attn: float32 [2048], P('head')
- grad_gain_ffn: float32 [2048], P('head')
- grad_w_gate: float32 [2048, 5632], P('seq', 'head')
- grad_w_up: float32 [2048, 5632], P('seq', 'head')
- grad_w_down: float32 [5632, 2048], P('head', 'seq')
All inputs are finite; a program needn't handle non-finite values.
Results may differ from a plain program's by a relative error of at most 0.017.
Values may be sent and summed in bfloat16 or wider, within the bound.
No kernel may reach another device: no remote copies, remote signals or barrier semaphores. Data moves between devices by JAX's collectives and lax.ppermute only.
A program may use at most 320 MiB of HBM per device.

v0:
```python
import jax
import jax.numpy as jnp
from jax import lax
from jax.sharding import PartitionSpec as P

HEAD_DIM = 128
KER = 4
SPAN = 128


norm_eps = 1e-06
highest = lax.Precision.HIGHEST


def passed_along(block, axis, distance):
    devices = range(lax.axis_size(axis))
    route = [(i - distance, i) for i in devices if i - distance in devices]
    return lax.ppermute(block, axis, route)


def prefix(part, axis, combine, identity, reverse):
    count = lax.axis_size(axis)
    place = lax.axis_index(axis)
    ahead = count - 1 - place if reverse else place
    gathered = jax.tree.map(lambda a: lax.all_gather(a, axis), part)
    state = jax.tree.map(lambda a, e: jnp.zeros_like(a) + jnp.asarray(e, a.dtype), part, identity)

    def one(turn, state):
        source = count - 1 - turn if reverse else turn
        return combine(
            state, jax.tree.map(lambda a: lax.dynamic_index_in_dim(a, source, 0, False), gathered)
        )

    return lax.fori_loop(0, ahead, one, state)


def rms_norm(v, gain):
    return v * lax.rsqrt(jnp.mean(v * v, axis=-1, keepdims=True) + norm_eps) * gain


def out_norm(mixer_out, values, gain):
    shaped = mixer_out.reshape(mixer_out.shape[:-1] + (-1, HEAD_DIM))
    scaled = shaped * lax.rsqrt(jnp.mean(shaped * shaped, axis=-1, keepdims=True) + norm_eps)
    return scaled.reshape(mixer_out.shape) * gain * jax.nn.silu(values)


def activate(q_conv, f_conv, i_conv, forget_gap):
    queries = jax.nn.silu(q_conv)
    key_in = forget_gap * jax.nn.sigmoid(-f_conv)
    log_decay = jnp.log1p(-key_in)
    return (queries, key_in, i_conv, log_decay)


def span_step(carried, pieces):
    memory, running = carried
    queries, key_in, values, log_decay = pieces
    cumulative = jnp.cumsum(log_decay, axis=-2)
    q_dec = queries * jnp.exp(cumulative)
    k_dec = key_in * jnp.exp(-cumulative)
    scores = jnp.einsum("...tk,...sk->...ts", q_dec, k_dec, precision=highest)
    length = queries.shape[-2]
    causal = jnp.arange(length)[:, None] >= jnp.arange(length)[None, :]
    scores = jnp.where(causal, scores, 0.0)
    outputs = jnp.einsum("...ts,...sv->...tv", scores, values, precision=highest)
    outputs = outputs + jnp.einsum("...tk,...kv->...tv", q_dec, memory, precision=highest)
    last_log = cumulative[..., -1, :]
    k_last = key_in * jnp.exp(last_log[..., None, :] - cumulative)
    memory = jnp.exp(last_log)[..., :, None] * memory + jnp.einsum(
        "...sk,...sv->...kv", k_last, values, precision=highest
    )
    q_total = q_dec * jnp.exp(running)[..., None, :]
    return ((memory, running + last_log), (outputs, q_total))


def local_states(queries, key_in, values, log_decay):
    batches, length, channels = queries.shape
    head_count = channels // HEAD_DIM
    block_count = length // SPAN

    def to_blocks(v):
        return v.reshape(batches, block_count, SPAN, head_count, HEAD_DIM).transpose(1, 0, 3, 2, 4)

    def from_blocks(v):
        return v.transpose(1, 0, 3, 2, 4).reshape(batches, length, channels)

    initial = (
        jnp.zeros((batches, head_count, HEAD_DIM, HEAD_DIM), jnp.float32),
        jnp.zeros((batches, head_count, HEAD_DIM), jnp.float32),
    )
    carried, stacked = lax.scan(
        jax.checkpoint(span_step),
        initial,
        (to_blocks(queries), to_blocks(key_in), to_blocks(values), to_blocks(log_decay)),
    )
    return (from_blocks(stacked[0]), from_blocks(stacked[1]), carried[0], jnp.exp(carried[1]))


def state_combine(earlier, later):
    early_decay, early_state = earlier
    late_decay, late_state = later
    return (early_decay * late_decay, late_state + late_decay[..., None] * early_state)


def short_conv(extended, kernel, length):
    result = kernel[0] * extended[:, 0:length]
    for offset in range(1, KER):
        result = result + kernel[offset] * extended[:, offset : offset + length]
    return result


def body(
    layer_input,
    w_q,
    w_f,
    w_i,
    conv_weight,
    forget_gap,
    gain_out,
    w_o,
    gain_attn,
    gain_ffn,
    w_gate,
    w_up,
    w_down,
    out_grad,
):
    inputs_full, attn_gain, ffn_gain, cot_full = (
        lax.all_gather(layer_input, "head", axis=2, tiled=True),
        lax.all_gather(gain_attn, "head", axis=0, tiled=True),
        lax.all_gather(gain_ffn, "head", axis=0, tiled=True),
        lax.all_gather(out_grad, "head", axis=2, tiled=True),
    )
    full_q, full_f, full_i, full_o, full_gate, full_up, full_down = (
        lax.all_gather(w_q, "seq", axis=0, tiled=True),
        lax.all_gather(w_f, "seq", axis=0, tiled=True),
        lax.all_gather(w_i, "seq", axis=0, tiled=True),
        lax.all_gather(w_o, "seq", axis=1, tiled=True),
        lax.all_gather(w_gate, "seq", axis=0, tiled=True),
        lax.all_gather(w_up, "seq", axis=0, tiled=True),
        lax.all_gather(w_down, "seq", axis=1, tiled=True),
    )
    batches = layer_input.shape[0]
    length = layer_input.shape[1]
    half_width = layer_input.shape[2]
    head_count = half_width // HEAD_DIM
    offset = lax.axis_index("head") * half_width
    x_full = inputs_full.astype(jnp.float32)
    normed_f32, norm1_pull = jax.vjp(rms_norm, x_full, attn_gain.astype(jnp.float32))
    normed = normed_f32.astype(jnp.bfloat16)
    w_proj = jnp.concatenate((full_q, full_f, full_i), axis=1)
    projected = jnp.einsum(
        "btd,de->bte", normed, w_proj, preferred_element_type=jnp.float32
    ).astype(jnp.bfloat16)
    previous = passed_along(projected[:, length - (KER - 1) :], "seq", 1)
    extended = jnp.concatenate((previous, projected), axis=1).astype(jnp.float32)
    kernel = conv_weight.astype(jnp.float32).transpose(1, 0, 2).reshape(KER, 3 * half_width)

    def conv_apply(source, taps):
        return short_conv(source, taps, length)

    conv_out, conv_pull = jax.vjp(conv_apply, extended, kernel)
    q_conv = conv_out[..., :half_width]
    f_conv = conv_out[..., half_width : 2 * half_width]
    i_conv = conv_out[..., 2 * half_width :]
    gap_f32 = forget_gap.astype(jnp.float32)

    def mixer_local(q_in, f_in, i_in, gap_in):
        return local_states(*activate(q_in, f_in, i_in, gap_in))

    (intra_out, q_total, final_state, block_decay), mixer_pull = jax.vjp(
        mixer_local, q_conv, f_conv, i_conv, gap_f32
    )
    unit_decay = jnp.ones_like(block_decay)
    zeros_state = jnp.zeros_like(final_state)
    prefix_decay, incoming = prefix(
        (block_decay, final_state), "seq", state_combine, (unit_decay, zeros_state), False
    )
    q_heads = q_total.reshape(batches, length, head_count, HEAD_DIM)
    mixer_out = intra_out + jnp.einsum(
        "bthk,bhkv->bthv", q_heads, incoming, precision=highest
    ).reshape(batches, length, half_width)
    gated_f32, gate_norm_pull = jax.vjp(out_norm, mixer_out, i_conv, gain_out.astype(jnp.float32))
    gated = gated_f32.astype(jnp.bfloat16)
    attn_part = jnp.einsum("btd,de->bte", gated, full_o, preferred_element_type=jnp.float32)
    attn_sum = lax.psum(attn_part.astype(jnp.bfloat16), "head").astype(jnp.float32)
    resid = x_full + attn_sum
    normed2_f32, norm2_pull = jax.vjp(rms_norm, resid, ffn_gain.astype(jnp.float32))
    normed2 = normed2_f32.astype(jnp.bfloat16)
    gate_pre = jnp.einsum("btd,df->btf", normed2, full_gate, preferred_element_type=jnp.float32)
    up_pre = jnp.einsum("btd,df->btf", normed2, full_up, preferred_element_type=jnp.float32)
    silu_gate = jax.nn.silu(gate_pre)
    hidden = (silu_gate * up_pre).astype(jnp.bfloat16)
    ffn_part = jnp.einsum("btf,fd->btd", hidden, full_down, preferred_element_type=jnp.float32)
    ffn_total = lax.psum_scatter(
        ffn_part.astype(jnp.bfloat16), "head", scatter_dimension=2, tiled=True
    ).astype(jnp.float32)
    resid_half = lax.dynamic_slice_in_dim(resid, offset, half_width, 2)
    output = (resid_half + ffn_total).astype(jnp.bfloat16)
    full_q, full_f, full_i, full_o, full_gate, full_up, full_down = (
        lax.all_gather(w_q, "seq", axis=0, tiled=True),
        lax.all_gather(w_f, "seq", axis=0, tiled=True),
        lax.all_gather(w_i, "seq", axis=0, tiled=True),
        lax.all_gather(w_o, "seq", axis=1, tiled=True),
        lax.all_gather(w_gate, "seq", axis=0, tiled=True),
        lax.all_gather(w_up, "seq", axis=0, tiled=True),
        lax.all_gather(w_down, "seq", axis=1, tiled=True),
    )
    w_proj = jnp.concatenate((full_q, full_f, full_i), axis=1)
    grad_w_down = jnp.einsum("btf,btd->fd", hidden, cot_full, preferred_element_type=jnp.float32)
    grad_hidden = jnp.einsum("btd,fd->btf", cot_full, full_down, preferred_element_type=jnp.float32)
    gate_sigmoid = jax.nn.sigmoid(gate_pre)
    grad_gate = (
        grad_hidden * up_pre * (gate_sigmoid * (1.0 + gate_pre * (1.0 - gate_sigmoid)))
    ).astype(jnp.bfloat16)
    grad_up = (grad_hidden * silu_gate).astype(jnp.bfloat16)
    grad_w_gate = jnp.einsum("btd,btf->df", normed2, grad_gate, preferred_element_type=jnp.float32)
    grad_w_up = jnp.einsum("btd,btf->df", normed2, grad_up, preferred_element_type=jnp.float32)
    grad_normed2 = jnp.einsum(
        "btf,df->btd", grad_gate, full_gate, preferred_element_type=jnp.float32
    )
    grad_normed2 = grad_normed2 + jnp.einsum(
        "btf,df->btd", grad_up, full_up, preferred_element_type=jnp.float32
    )
    grad_normed2 = lax.psum(grad_normed2.astype(jnp.bfloat16), "head").astype(jnp.float32)
    grad_resid_norm, grad_ffn_gain = norm2_pull(grad_normed2)
    grad_resid = cot_full.astype(jnp.float32) + grad_resid_norm
    grad_attn = grad_resid.astype(jnp.bfloat16)
    grad_w_o = jnp.einsum("btd,bte->de", gated, grad_attn, preferred_element_type=jnp.float32)
    grad_gated = jnp.einsum("bte,de->btd", grad_attn, full_o, preferred_element_type=jnp.float32)
    grad_mixer, grad_gate_src, grad_gain_out = gate_norm_pull(grad_gated)
    grad_mixer_heads = grad_mixer.reshape(batches, length, head_count, HEAD_DIM)
    grad_q_heads = jnp.einsum("bthv,bhkv->bthk", grad_mixer_heads, incoming, precision=highest)
    grad_incoming = jnp.einsum("bthk,bthv->bhkv", q_heads, grad_mixer_heads, precision=highest)
    later_decay, grad_final = prefix(
        (block_decay, grad_incoming), "seq", state_combine, (unit_decay, zeros_state), True
    )
    grad_decay = jnp.sum(incoming * grad_final, axis=-1)
    grad_q_conv, grad_f_conv, grad_i_conv, grad_gap = mixer_pull(
        (grad_mixer, grad_q_heads.reshape(batches, length, half_width), grad_final, grad_decay)
    )
    grad_conv_out = jnp.concatenate(
        (grad_q_conv, grad_f_conv, grad_i_conv + grad_gate_src), axis=-1
    )
    grad_extended, grad_kernel = conv_pull(grad_conv_out)
    sent_back = passed_along(grad_extended[:, : KER - 1].astype(jnp.bfloat16), "seq", -1).astype(
        jnp.float32
    )
    grad_own = grad_extended[:, KER - 1 :]
    grad_proj = jnp.concatenate(
        (grad_own[:, : length - (KER - 1)], grad_own[:, length - (KER - 1) :] + sent_back), axis=1
    ).astype(jnp.bfloat16)
    grad_w_proj = jnp.einsum("btd,bte->de", normed, grad_proj, preferred_element_type=jnp.float32)
    grad_normed = jnp.einsum("bte,de->btd", grad_proj, w_proj, preferred_element_type=jnp.float32)
    grad_normed = lax.psum(grad_normed.astype(jnp.bfloat16), "head").astype(jnp.float32)
    grad_x_norm, grad_attn_gain = norm1_pull(grad_normed)
    grad_x = grad_resid + grad_x_norm
    input_grad = lax.dynamic_slice_in_dim(grad_x, offset, half_width, 2).astype(jnp.bfloat16)
    summed = (
        lax.psum_scatter(grad_w_proj[:, :half_width], "seq", scatter_dimension=0, tiled=True),
        lax.psum_scatter(
            grad_w_proj[:, half_width : 2 * half_width], "seq", scatter_dimension=0, tiled=True
        ),
        lax.psum_scatter(grad_w_proj[:, 2 * half_width :], "seq", scatter_dimension=0, tiled=True),
        lax.psum_scatter(grad_w_o, "seq", scatter_dimension=1, tiled=True),
        lax.psum_scatter(grad_w_gate, "seq", scatter_dimension=0, tiled=True),
        lax.psum_scatter(grad_w_up, "seq", scatter_dimension=0, tiled=True),
        lax.psum_scatter(grad_w_down, "seq", scatter_dimension=1, tiled=True),
    )
    grad_conv_local = grad_kernel.reshape(KER, 3, half_width).transpose(1, 0, 2)
    attn_gain_half = lax.dynamic_slice_in_dim(grad_attn_gain, offset, half_width, 0)
    ffn_gain_half = lax.dynamic_slice_in_dim(grad_ffn_gain, offset, half_width, 0)
    small_sums = lax.psum(
        (grad_conv_local, grad_gap, grad_gain_out, attn_gain_half, ffn_gain_half), "seq"
    )
    return (
        output,
        input_grad,
        summed[0],
        summed[1],
        summed[2],
        small_sums[0],
        small_sums[1],
        small_sums[2],
        summed[3],
        small_sums[3],
        small_sums[4],
        summed[4],
        summed[5],
        summed[6],
    )


def solution(mesh):
    placed = (
        P(None, "seq", "head"),
        P("seq", "head"),
        P("seq", "head"),
        P("seq", "head"),
        P(None, None, "head"),
        P("head"),
        P("head"),
        P("head", "seq"),
        P("head"),
        P("head"),
        P("seq", "head"),
        P("seq", "head"),
        P("head", "seq"),
        P(None, "seq", "head"),
    )
    return jax.shard_map(
        body,
        mesh=mesh,
        in_specs=placed,
        out_specs=(
            P(None, "seq", "head"),
            P(None, "seq", "head"),
            P("seq", "head"),
            P("seq", "head"),
            P("seq", "head"),
            P(None, None, "head"),
            P("head"),
            P("head"),
            P("head", "seq"),
            P("head"),
            P("head"),
            P("seq", "head"),
            P("seq", "head"),
            P("head", "seq"),
        ),
        check_vma=False,
    )
```

profile of v0, /device:TPU:0, one launch (start us, length us, event | category | flops | bytes accessed | tf_op | source)
XLA Modules:
  0.0 4503.1 jit_solution(16265099138296379249)
XLA Ops:
  25.9 71.2 %all-gather.21.cloned.1.call-done = bf16[2048,1024]{1,0:T(8,128)(2,1)} async-done(((bf16[32,1024]{1,0:T(8,128)(2,1)}), bf16[2048,1024]{1,0:T(8,128)(2,1)}) %all-gather.21.cloned.1.call-update) | async-done | bytes 4194320 | tf_op jit(solution)/shard_map/all_gather | solution.py:136
  97.2 69.4 %all-gather.19.cloned.1.call-done = bf16[2048,1024]{1,0:T(8,128)(2,1)} async-done(((bf16[32,1024]{1,0:T(8,128)(2,1)}), bf16[2048,1024]{1,0:T(8,128)(2,1)}) %all-gather.19.cloned.1.call-update) | async-done | bytes 4194320 | tf_op jit(solution)/shard_map/all_gather | solution.py:135
  166.5 69.2 %all-gather.17.cloned.1.call-done = bf16[2048,1024]{1,0:T(8,128)(2,1)} async-done(((bf16[32,1024]{1,0:T(8,128)(2,1)}), bf16[2048,1024]{1,0:T(8,128)(2,1)}) %all-gather.17.cloned.1.call-update) | async-done | bytes 4194320 | tf_op jit(solution)/shard_map/all_gather | solution.py:134
  272.6 191.3 %all-gather.1 = f32[128,8,1,128]{3,1,2,0:T(8,128)} all-gather(f32[2,8,1,128]{3,1,2,0:T(8,128)S(1)} %get-tuple-element.307), channel_id=3, replica_groups=mesh['seq'=64,'head'=2] {'seq'}, dimensions={0}, use_global_device_ids=true | all-gather | bytes 532480 | tf_op jit(solution)/shard_map/all_gather | solution.py:25
  473.1 77.0 %all-gather.33.cloned.1.call-done = f32[128,8,128,128]{3,2,1,0:T(8,128)} async-done(((f32[2,8,128,128]{3,2,1,0:T(8,128)}), f32[128,8,128,128]{3,2,1,0:T(8,128)}) %all-gather.33.cloned.1.call-update) | async-done | bytes 67108880 | tf_op jit(solution)/shard_map/all_gather | solution.py:25
  562.6 57.8 %all-gather.23.cloned.1.call-done = bf16[1024,2048]{0,1:T(8,128)(2,1)} async-done(((bf16[1024,32]{0,1:T(8,128)(2,1)}), bf16[1024,2048]{0,1:T(8,128)(2,1)}) %all-gather.23.cloned.1.call-update) | async-done | bytes 4194320 | tf_op jit(solution)/shard_map/all_gather | solution.py:137
  631.3 92.4 %all-gather.29.cloned.1.call-done = bf16[2816,2048]{0,1:T(8,128)(2,1)} async-done(((bf16[2816,32]{0,1:T(8,128)(2,1)}), bf16[2816,2048]{0,1:T(8,128)(2,1)}) %all-gather.29.cloned.1.call-update) | async-done | bytes 11534352 | tf_op jit(solution)/shard_map/all_gather | solution.py:140
  733.0 83.6 %all-reduce.15.cloned.1.call-done = bf16[2,128,2048]{2,1,0:T(8,128)(2,1)} async-done(((bf16[2,128,2048]{2,1,0:T(8,128)(2,1)}), bf16[2,128,2048]{2,1,0:T(8,128)(2,1)}) %all-reduce.15.cloned.1.call-update) | async-done | bytes 1048592 | tf_op jit(solution)/shard_map/psum | solution.py:185
  821.5 87.7 %all-gather.27.cloned.1.call-done = bf16[2048,2816]{1,0:T(8,128)(2,1)} async-done(((bf16[32,2816]{1,0:T(8,128)(2,1)}), bf16[2048,2816]{1,0:T(8,128)(2,1)}) %all-gather.27.cloned.1.call-update) | async-done | bytes 11534352 | tf_op jit(solution)/shard_map/all_gather | solution.py:139
  918.5 81.6 %all-gather.25.cloned.1.call-done = bf16[2048,2816]{1,0:T(8,128)(2,1)} async-done(((bf16[32,2816]{1,0:T(8,128)(2,1)}), bf16[2048,2816]{1,0:T(8,128)(2,1)}) %all-gather.25.cloned.1.call-update) | async-done | bytes 11534352 | tf_op jit(solution)/shard_map/all_gather | solution.py:138
  1000.2 11.3 multiply_convert_fusion.1
  1027.1 24.8 all-reduce.17.cloned.1.call-done
  1077.4 274.4 %all-gather.35.cloned.1.call-done = f32[128,8,128,128]{3,2,1,0:T(8,128)} async-done(((f32[2,8,128,128]{3,2,1,0:T(8,128)}), f32[128,8,128,128]{3,2,1,0:T(8,128)}) %all-gather.35.cloned.1.call-update) | async-done | bytes 67108880 | tf_op jit(solution)/shard_map/all_gather | solution.py:25
  1352.9 223.3 %while.17 = (s32[]{:T(128)}, f32[2,8,128,128]{3,2,1,0:T(8,128)}, s32[]{:T(128)}, f32[64,2,8,128,128]{4,3,2,1,0:T(8,128)}, f32[64,2,8,128]{3,2,1,0:T(8,128)}, /*index=5*/s32[]{:T(128)}, s32[]{:T(128)}, s32[]{:T(128)}, s32[]{:T(128)}) while((s32[]{:T(128)}, f32[2,8,128,128]{3,2,1,0:T(8,128)}, s32[]{:T(128)}, ...), condition=%wide.region_12.13_spmd, body=%wide.region_11.12_spmd.sunk | while | flops 524294 | bytes 3170459 | solution.py:34
  1706.2 11.7 convolution_bitcast_fusion.1
  1721.9 18.2 fusion.86
  1748.2 312.4 %reduce-scatter.17.cloned.1.call-done = f32[1024,32]{0,1:T(8,128)} async-done(((f32[1024,2048]{0,1:T(8,128)}), f32[1024,32]{0,1:T(8,128)}) %reduce-scatter.17.cloned.1.call-update) | async-done | bytes 131088 | tf_op jit(solution)/shard_map/reduce_scatter | solution.py:264
  2060.6 399.2 %reduce-scatter.19.cloned.1.call-done = f32[32,2816]{1,0:T(8,128)} async-done(((f32[2048,2816]{1,0:T(8,128)}), f32[32,2816]{1,0:T(8,128)}) %reduce-scatter.19.cloned.1.call-update) | async-done | bytes 360464 | tf_op jit(solution)/shard_map/reduce_scatter | solution.py:265
  2459.8 400.1 %reduce-scatter.21.cloned.1.call-done = f32[32,2816]{1,0:T(8,128)} async-done(((f32[2048,2816]{1,0:T(8,128)}), f32[32,2816]{1,0:T(8,128)}) %reduce-scatter.21.cloned.1.call-update) | async-done | bytes 360464 | tf_op jit(solution)/shard_map/reduce_scatter | solution.py:266
  2859.9 401.7 %reduce-scatter.23.cloned.1.call-done = f32[2816,32]{0,1:T(8,128)} async-done(((f32[2816,2048]{0,1:T(8,128)}), f32[2816,32]{0,1:T(8,128)}) %reduce-scatter.23.cloned.1.call-update) | async-done | bytes 360464 | tf_op jit(solution)/shard_map/reduce_scatter | solution.py:267
  3261.5 126.4 %all-reduce.21.cloned.1.call-done = (f32[3,4,1024]{2,1,0:T(4,128)}, f32[1024]{0:T(1024)}, f32[1024]{0:T(1024)}, f32[1024]{0:T(1024)}, f32[1024]{0:T(1024)}) async-done(((f32[3,4,1024]{2,1,0:T(4,128)}, f32[1024]{0:T(1024)}, f32[1024]{0:T(1024)}, f32[1024]{0:T(1024)}, f32[1024]{0:T(1024)}), (f32[3,4,1024]{2,1,0:T(4,128)}, f32[1024]{0:T(1024)}, f32[1024]{0:T(1024)}, f32[1024]{0:T(1024)}, ...) | async-done | bytes 65552 | tf_op jit(solution)/shard_map/psum | solution.py:272
  3388.0 370.4 %reduce-scatter.11.cloned.1.call-done = f32[32,1024]{1,0:T(8,128)} async-done(((f32[2048,1024]{1,0:T(8,128)}), f32[32,1024]{1,0:T(8,128)}) %reduce-scatter.11.cloned.1.call-update) | async-done | bytes 131088 | tf_op jit(solution)/shard_map/reduce_scatter | solution.py:259
  3758.4 366.0 %reduce-scatter.13.cloned.1.call-done = f32[32,1024]{1,0:T(8,128)} async-done(((f32[2048,1024]{1,0:T(8,128)}), f32[32,1024]{1,0:T(8,128)}) %reduce-scatter.13.cloned.1.call-update) | async-done | bytes 131088 | tf_op jit(solution)/shard_map/reduce_scatter | solution.py:260
  4124.4 365.4 %reduce-scatter.15.cloned.1.call-done = f32[32,1024]{1,0:T(8,128)} async-done(((f32[2048,1024]{1,0:T(8,128)}), f32[32,1024]{1,0:T(8,128)}) %reduce-scatter.15.cloned.1.call-update) | async-done | bytes 131088 | tf_op jit(solution)/shard_map/reduce_scatter | solution.py:263
  (377 shorter events, 524.6 us)
Async XLA Ops:
  7.2 16.7 all-gather.15.cloned.1.call-start
  7.9 89.3 %all-gather.21.cloned.1.call-start = ((), (), s32[]{:S(2)}) async-start(), calls=%async_computation.11 | async-start | bytes 4259840 | tf_op jit(solution)/shard_map/all_gather | solution.py:136
  8.7 157.9 %all-gather.19.cloned.1.call-start = ((), (), s32[]{:S(2)}) async-start(), calls=%async_computation.10 | async-start | bytes 4259840 | tf_op jit(solution)/shard_map/all_gather | solution.py:135
  9.4 226.4 %all-gather.17.cloned.1.call-start = ((), (), s32[]{:S(2)}) async-start(), calls=%async_computation.9 | async-start | bytes 4259840 | tf_op jit(solution)/shard_map/all_gather | solution.py:134
  10.0 540.2 %all-gather.33.cloned.1.call-start = ((), (), s32[]{:S(2)}) async-start(), calls=%async_computation.28 | async-start | bytes 68157440 | tf_op jit(solution)/shard_map/all_gather | solution.py:25
  267.9 352.6 %all-gather.23.cloned.1.call-start = ((), (), s32[]{:S(2)}) async-start(), calls=%async_computation.12 | async-start | bytes 4259840 | tf_op jit(solution)/shard_map/all_gather | solution.py:137
  268.4 362.8 %all-gather.31.cloned.1.call-start = ((), (), s32[]{:S(2)}) async-start(), calls=%async_computation.18 | async-start | bytes 1572864 | tf_op jit(solution)/shard_map/all_gather | solution.py:131
  269.2 454.4 %all-gather.29.cloned.1.call-start = ((), (), s32[]{:S(2)}) async-start(), calls=%async_computation.16 | async-start | bytes 11714560 | tf_op jit(solution)/shard_map/all_gather | solution.py:140
  269.9 546.6 %all-reduce.15.cloned.1.call-start = ((), (), s32[]{:S(2)}) async-start(), calls=%async_computation.13 | async-start | bytes 2097152 | tf_op jit(solution)/shard_map/psum | solution.py:185
  625.2 284.0 %all-gather.27.cloned.1.call-start = ((), (), s32[]{:S(2)}) async-start(), calls=%async_computation.15 | async-start | bytes 11714560 | tf_op jit(solution)/shard_map/all_gather | solution.py:139
  625.8 374.4 %all-gather.25.cloned.1.call-start = ((), (), s32[]{:S(2)}) async-start(), calls=%async_computation.14 | async-start | bytes 11714560 | tf_op jit(solution)/shard_map/all_gather | solution.py:138
  626.5 425.4 %all-reduce.17.cloned.1.call-start = ((), (), s32[]{:S(2)}) async-start(), calls=%async_computation.19 | async-start | bytes 2097152 | tf_op jit(solution)/shard_map/psum | solution.py:224
  1027.1 324.7 %all-gather.35.cloned.1.call-start = ((), (), s32[]{:S(2)}) async-start(), calls=%async_computation.29 | async-start | bytes 68157440 | tf_op jit(solution)/shard_map/all_gather | solution.py:25
  1073.7 644.2 %all-reduce.19.cloned.1.call-start = ((), (), s32[]{:S(2)}) async-start(), calls=%async_computation.20 | async-start | bytes 2097152 | tf_op jit(solution)/shard_map/psum | solution.py:254
  1641.6 6.0 collective-permute-start.1
  1655.0 88.2 %reduce-scatter.9.cloned.1.call-start = ((), (), s32[]{:S(2)}) async-start(), calls=%async_computation.17 | async-start | bytes 1572864 | tf_op jit(solution)/shard_map/reduce_scatter | solution.py:194
  1664.8 395.8 %reduce-scatter.17.cloned.1.call-start = ((), (), s32[]{:S(2)}) async-start(), calls=%async_computation.24 | async-start | bytes 8519680 | tf_op jit(solution)/shard_map/reduce_scatter | solution.py:264
  1669.6 790.2 %reduce-scatter.19.cloned.1.call-start = ((), (), s32[]{:S(2)}) async-start(), calls=%async_computation.25 | async-start | bytes 23429120 | tf_op jit(solution)/shard_map/reduce_scatter | solution.py:265
  1681.7 1178.2 %reduce-scatter.21.cloned.1.call-start = ((), (), s32[]{:S(2)}) async-start(), calls=%async_computation.26 | async-start | bytes 23429120 | tf_op jit(solution)/shard_map/reduce_scatter | solution.py:266
  1692.7 1568.8 %reduce-scatter.23.cloned.1.call-start = ((), (), s32[]{:S(2)}) async-start(), calls=%async_computation.27 | async-start | bytes 23429120 | tf_op jit(solution)/shard_map/reduce_scatter | solution.py:267
  1704.9 1683.1 %all-reduce.21.cloned.1.call-start = ((), (), s32[]{:S(2)}) async-start(), calls=%async_computation.30 | async-start | bytes 131072 | tf_op jit(solution)/shard_map/psum | solution.py:272
  1721.9 2036.6 %reduce-scatter.11.cloned.1.call-start = ((), (), s32[]{:S(2)}) async-start(), calls=%async_computation.21 | async-start | bytes 8519680 | tf_op jit(solution)/shard_map/reduce_scatter | solution.py:259
  1740.2 2384.3 %reduce-scatter.13.cloned.1.call-start = ((), (), s32[]{:S(2)}) async-start(), calls=%async_computation.22 | async-start | bytes 8519680 | tf_op jit(solution)/shard_map/reduce_scatter | solution.py:260
  1740.9 2748.9 %reduce-scatter.15.cloned.1.call-start = ((), (), s32[]{:S(2)}) async-start(), calls=%async_computation.23 | async-start | bytes 8519680 | tf_op jit(solution)/shard_map/reduce_scatter | solution.py:263
  (47 other events, 1082.8 us)
Sparse Core Ops, SparseCore 0:
  9.7 14.1 all-gather.14
  26.7 70.3 all-gather.20
  100.0 66.4 all-gather.18
  169.3 66.4 all-gather.16
  268.0 282.0 all-gather.32
  552.9 67.5 all-gather.22
  622.1 9.1 all-gather.30
  634.1 89.4 all-gather.28
  726.1 90.4 all-reduce.14
  819.7 89.4 all-gather.26
  912.5 87.6 all-gather.24
  1027.2 24.6 all-reduce.16
  1073.8 277.9 all-gather.34
  1655.2 18.4 all-reduce.18
  1676.0 12.4 reduce-scatter.8
  1691.3 369.2 reduce-scatter.16
  2063.4 396.3 reduce-scatter.18
  2462.6 397.2 reduce-scatter.20
  2862.9 398.6 reduce-scatter.22
  3268.0 119.8 all-reduce.20
  3391.1 367.3 reduce-scatter.10
  3761.5 362.8 reduce-scatter.12
  4127.5 362.2 reduce-scatter.14
where the time goes:
time: 4510 us; the launch traced here: 4500 us
  waiting for transfers between devices  3760 us (83%)
  other arithmetic  237 us (5%)
  blocking collectives  195 us (4%)
  matrix products  180 us (4%)
  local copies, waits for them, and re-layouts  113 us (3%)
    reduce_scatter x1, waiting for transfers between devices, body(): lax.psum_scatter(grad_w_down, 'seq', scatter_dimension=1, tiled=True)  402 us
    reduce_scatter x1, waiting for transfers between devices, body(): lax.psum_scatter(grad_w_up, 'seq', scatter_dimension=0, tiled=True)  400 us
    reduce_scatter x1, waiting for transfers between devices, body(): lax.psum_scatter(grad_w_gate, 'seq', scatter_dimension=0, tiled=True)  399 us
    reduce_scatter x1, waiting for transfers between devices, body(): lax.psum_scatter(grad_w_proj[:, :half_width], 'seq', scatter_dimension=0,...  370 us
    reduce_scatter x1, waiting for transfers between devices, body(): lax.psum_scatter(grad_w_proj[:, half_width:2 * half_width], 'seq', scatte...  366 us
    reduce_scatter x1, waiting for transfers between devices, body(): lax.psum_scatter(grad_w_proj[:, 2 * half_width:], 'seq', scatter_dimensio...  365 us
    all_gather x2, waiting for transfers between devices, prefix(): gathered = jax.tree.map(lambda a: lax.all_gather(a, axis), part)  351 us
    reduce_scatter x1, waiting for transfers between devices, body(): lax.psum_scatter(grad_w_o, 'seq', scatter_dimension=1, tiled=True)  312 us
  transfers between devices with their start and end apart: 25, of which 23 were waited for; matrix products, arithmetic and copies ran while one was open for 3% of the time, Pallas kernels for 0%

commit v1 on v0

v1 whole, which is shorter than its diff:
```python
import jax
import jax.numpy as jnp
from jax import lax
from jax.sharding import Mesh
from jax.sharding import PartitionSpec as P

HEAD_DIM = 128
KER = 4
SPAN = 128
RING = 4
PLANE = ("x", "z")
SEQ = ("x", "z", "y")

norm_eps = 1e-06
highest = lax.Precision.HIGHEST
f32 = jnp.float32
bf16 = jnp.bfloat16


def swap(block):
    return lax.ppermute(block, "head", [(0, 1), (1, 0)])


def exchange(block, axis):
    return lax.all_to_all(block, axis, 0, 0, tiled=True)


def gather_y(block):
    return exchange(jnp.broadcast_to(block[None], (RING,) + block.shape), "y")


def scatter_y(blocks):
    return jnp.sum(exchange(blocks, "y").astype(f32), axis=0)


def dot(a, b, contract):
    return lax.dot_general(a, b, (contract, ((), ())), preferred_element_type=f32)


def to_sequence(block, head):
    mine = lax.dynamic_index_in_dim(block, head, 0, False)
    other = swap(lax.dynamic_index_in_dim(block, 1 - head, 0, False))
    first = head == 0
    return jnp.concatenate((jnp.where(first, mine, other), jnp.where(first, other, mine)), axis=1)


def from_sequence(block, head):
    half = block.shape[1] // 2
    mine = lax.dynamic_slice_in_dim(block, head * half, half, 1)
    other = swap(lax.dynamic_slice_in_dim(block, (1 - head) * half, half, 1))
    first = head == 0
    return jnp.stack((jnp.where(first, mine, other), jnp.where(first, other, mine)))


def rms_norm(v, gain):
    return v * lax.rsqrt(jnp.mean(v * v, axis=-1, keepdims=True) + norm_eps) * gain


def out_norm(mixer_out, values, gain):
    scaled = mixer_out * lax.rsqrt(jnp.mean(mixer_out * mixer_out, axis=-1, keepdims=True) + norm_eps)
    return scaled * gain * jax.nn.silu(values)


def activate(q_conv, f_conv, i_conv, forget_gap):
    queries = jax.nn.silu(q_conv)
    key_in = forget_gap * jax.nn.sigmoid(-f_conv)
    log_decay = jnp.log1p(-key_in)
    return (queries, key_in, i_conv, log_decay)


def ein(form, a, b):
    return jnp.einsum(form, a, b, precision=highest)


def group_prefix(decay, state, reverse):
    groups = lax.axis_size(PLANE)
    heads, keys, width = state.shape
    rows = keys // groups
    packed = jnp.concatenate(
        (
            state.reshape(heads, groups, rows, width),
            jnp.broadcast_to(decay.reshape(heads, groups, rows, 1), (heads, groups, rows, width)),
        ),
        axis=2,
    ).transpose(1, 0, 2, 3)
    held = exchange(packed, PLANE)
    states, decays = held[:, :, :rows], held[:, :, rows:]
    order = range(groups - 1, -1, -1) if reverse else range(groups)
    entering = [None] * groups
    running = jnp.zeros_like(states[0])
    for g in order:
        entering[g] = running
        running = states[g] + decays[g] * running
    back = exchange(jnp.stack(entering), PLANE)
    return back.transpose(1, 0, 2, 3).reshape(heads, keys, width)


def short_conv(extended, kernel, length):
    result = kernel[0] * extended[0:length]
    for offset in range(1, KER):
        result = result + kernel[offset] * extended[offset : offset + length]
    return result


def gather_rows(packed):
    held = exchange(packed, "y")
    held = held.reshape((RING * packed.shape[1],) + packed.shape[2:])
    return lax.all_gather(held, PLANE, axis=0, tiled=True)


def for_y(w):
    rows, columns = w.shape
    return w.reshape(rows, RING, columns // RING).transpose(1, 0, 2)


def body(
    layer_input,
    w_q,
    w_f,
    w_i,
    conv_weight,
    forget_gap,
    gain_out,
    w_o,
    gain_attn,
    gain_ffn,
    w_gate,
    w_up,
    w_down,
    out_grad,
):
    head = lax.axis_index("head")
    place = lax.axis_index("y")
    groups = lax.axis_size(PLANE)
    length = layer_input.shape[1]
    width = 2 * layer_input.shape[2]
    slice_width = w_q.shape[1] // RING
    ff_slice = w_gate.shape[1] // RING
    tokens = RING * length

    attn_packed = jnp.concatenate((for_y(w_q), for_y(w_f), for_y(w_i)), axis=2)
    proj_a = gather_rows(attn_packed)
    w_ot = w_o.T
    o_a = lax.all_gather(
        gather_y(w_ot).reshape(RING * w_ot.shape[0], w_ot.shape[1]), PLANE, axis=0, tiled=True
    )
    ff_packed = jnp.stack((for_y(w_gate), for_y(w_up), for_y(w_down.T)), axis=1)
    held = exchange(ff_packed, "y").transpose(1, 0, 2, 3).reshape(3, -1, ff_slice)
    ff_a = lax.all_gather(held, PLANE, axis=1, tiled=True)
    proj_b, o_b, ff_b = swap(proj_a), swap(o_a), swap(ff_a)

    def channel_slice(v):
        own = lax.dynamic_slice_in_dim(v, place * slice_width, slice_width, v.ndim - 1)
        return own

    small_own = jnp.concatenate(
        (
            channel_slice(conv_weight).reshape(3 * KER, slice_width),
            channel_slice(forget_gap)[None],
            channel_slice(gain_out)[None],
        )
    )
    small = jnp.concatenate((small_own, swap(small_own)), axis=1).astype(f32)
    heads = 2 * slice_width // HEAD_DIM
    conv_k = small[: 3 * KER].reshape(3, KER, 2 * slice_width)
    gap = small[3 * KER].reshape(heads, 1, 1, HEAD_DIM)
    gain_o = small[3 * KER + 1].reshape(heads, 1, 1, HEAD_DIM)
    gains_own = jnp.stack((gain_attn, gain_ffn))
    gains_other = swap(gains_own)
    gains = jnp.where(
        head == 0,
        jnp.concatenate((gains_own, gains_other), axis=1),
        jnp.concatenate((gains_other, gains_own), axis=1),
    ).astype(f32)
    g_attn, g_ffn = gains[0], gains[1]

    x_own = to_sequence(layer_input, head)
    dy_own = to_sequence(out_grad, head)
    x_all = gather_y(x_own).reshape(tokens, width).astype(f32)
    dy_all = gather_y(dy_own).reshape(tokens, width)
    normed = rms_norm(x_all, g_attn).astype(bf16)

    c_rows = ((1,), (0,))
    c_cols = ((1,), (1,))
    c_toks = ((0,), (0,))
    projected = jnp.concatenate(
        [dot(normed, w, c_rows).astype(bf16).reshape(tokens, 3, slice_width) for w in (proj_a, proj_b)],
        axis=2,
    )
    route = [(i, i + 1) for i in range(groups - 1)]
    before = lax.ppermute(projected[tokens - (KER - 1) :], PLANE, route)
    extended = jnp.concatenate((before, projected)).astype(f32)
    taps = conv_k.transpose(1, 0, 2)
    conv_out, conv_pull = jax.vjp(lambda e, k: short_conv(e, k, tokens), extended, taps)

    def units(v):
        return v.reshape(RING, SPAN, heads, HEAD_DIM).transpose(2, 0, 1, 3)

    def from_units(v):
        return v.transpose(1, 2, 0, 3).reshape(tokens, heads * HEAD_DIM)

    (queries, key_in, values, log_decay), act_pull = jax.vjp(
        activate, units(conv_out[:, 0]), units(conv_out[:, 1]), units(conv_out[:, 2]), gap
    )
    cumulative = jnp.cumsum(log_decay, axis=-2)
    last_log = cumulative[..., -1:, :]
    grow = jnp.exp(cumulative)
    shrink = jnp.exp(-cumulative)
    rest = jnp.exp(last_log - cumulative)
    q_dec = queries * grow
    k_dec = key_in * shrink
    k_last = key_in * rest
    block_decay = jnp.exp(last_log[..., 0, :])
    causal = jnp.arange(SPAN)[:, None] >= jnp.arange(SPAN)[None, :]
    added = ein("hnsk,hnsv->hnkv", k_last, values)
    local = jnp.zeros_like(added[:, 0])
    for n in range(RING):
        local = added[:, n] + block_decay[:, n, :, None] * local
    group_decay = jnp.prod(block_decay, axis=1)
    state = group_prefix(group_decay, local, False)
    scores = jnp.where(causal, ein("hntk,hnsk->hnts", q_dec, k_dec), 0.0)
    intra = ein("hnts,hnsv->hntv", scores, values)
    entering = []
    for n in range(RING):
        entering.append(state)
        state = added[:, n] + block_decay[:, n, :, None] * state
    entering = jnp.stack(entering, axis=1)
    mixer_out = intra + ein("hntk,hnkv->hntv", q_dec, entering)
    gated_f32, gate_norm_pull = jax.vjp(out_norm, mixer_out, values, gain_o)
    gated = from_units(gated_f32.astype(bf16))

    gathered = gather_y(gated).reshape(RING, tokens, 2, slice_width)

    def all_channels(half):
        return gathered[:, :, half].transpose(1, 0, 2).reshape(tokens, RING * slice_width)

    attn_sum = dot(all_channels(0), o_a, c_cols) + dot(all_channels(1), o_b, c_cols)
    resid = x_all + attn_sum
    normed2 = rms_norm(resid, g_ffn).astype(bf16)

    ffn_part = 0.0
    grad_normed2 = 0.0
    ff_grads = []
    for ff in (ff_a, ff_b):
        gate_w, up_w, down_t = ff[0], ff[1], ff[2]
        grad_hidden = dot(dy_all, down_t, c_rows)
        gate_pre = dot(normed2, gate_w, c_rows)
        up_pre = dot(normed2, up_w, c_rows)
        sig = jax.nn.sigmoid(gate_pre)
        silu_gate = gate_pre * sig
        hidden = (silu_gate * up_pre).astype(bf16)
        grad_gate = (grad_hidden * up_pre * (sig * (1.0 + gate_pre * (1.0 - sig)))).astype(bf16)
        grad_up = (grad_hidden * silu_gate).astype(bf16)
        grad_normed2 = grad_normed2 + dot(grad_gate, gate_w, c_cols) + dot(grad_up, up_w, c_cols)
        ffn_part = ffn_part + dot(hidden, down_t, c_cols)
        ff_grads.append(
            jnp.stack(
                [
                    dot(a, b, c_toks).astype(bf16)
                    for a, b in ((normed2, grad_gate), (normed2, grad_up), (dy_all, hidden))
                ]
            )
        )

    def split_tokens(v):
        return v.astype(bf16).reshape(RING, length, width)

    def own_tokens(v):
        return lax.dynamic_slice_in_dim(v, place * length, length, 0)

    resid_own = own_tokens(resid)
    grad_normed2 = scatter_y(split_tokens(grad_normed2))
    _, norm2_pull = jax.vjp(rms_norm, resid_own, g_ffn)
    grad_resid_norm, grad_g_ffn = norm2_pull(grad_normed2)
    grad_resid = dy_own.astype(f32) + grad_resid_norm
    grad_attn_own = grad_resid.astype(bf16)
    grad_attn = gather_y(grad_attn_own).reshape(tokens, width)

    output = (resid_own + scatter_y(split_tokens(ffn_part))).astype(bf16)
    output = from_sequence(output, head)

    def o_slice(w):
        return lax.dynamic_slice_in_dim(w, place * slice_width, slice_width, 1)

    grad_gated = jnp.concatenate([dot(grad_attn, o_slice(w), c_rows) for w in (o_a, o_b)], axis=1)
    grad_mixer, grad_values_gate, grad_gain_o = gate_norm_pull(units(grad_gated))
    added_back = ein("hntk,hntv->hnkv", q_dec, grad_mixer)
    local = jnp.zeros_like(added_back[:, 0])
    for n in range(RING - 1, -1, -1):
        local = added_back[:, n] + block_decay[:, n, :, None] * local
    grad_state = group_prefix(group_decay, local, True)
    leaving = [None] * RING
    for n in range(RING - 1, -1, -1):
        leaving[n] = grad_state
        grad_state = added_back[:, n] + block_decay[:, n, :, None] * grad_state
    leaving = jnp.stack(leaving, axis=1)
    grad_scores = jnp.where(causal, ein("hntv,hnsv->hnts", grad_mixer, values), 0.0)
    grad_q_dec = ein("hnts,hnsk->hntk", grad_scores, k_dec) + ein("hntv,hnkv->hntk", grad_mixer, entering)
    grad_k_dec = ein("hnts,hntk->hnsk", grad_scores, q_dec)
    grad_values = ein("hnts,hntv->hnsv", scores, grad_mixer) + ein("hnsk,hnkv->hnsv", k_last, leaving)
    grad_k_last = ein("hnsv,hnkv->hnsk", values, leaving)
    grad_block_decay = jnp.sum(entering * leaving, axis=-1)
    through_last = grad_k_last * k_last
    grad_cumulative = grad_q_dec * q_dec - grad_k_dec * k_dec - through_last
    grad_last = jnp.sum(through_last, axis=-2) + grad_block_decay * block_decay
    grad_log = lax.cumsum(grad_cumulative, axis=2, reverse=True) + grad_last[:, :, None, :]
    grad_queries = grad_q_dec * grow
    grad_key = grad_k_dec * shrink + grad_k_last * rest
    grad_q, grad_f, grad_i, grad_gap = act_pull(
        (grad_queries, grad_key, grad_values + grad_values_gate, grad_log)
    )
    grad_conv_out = jnp.stack([from_units(v) for v in (grad_q, grad_f, grad_i)], axis=1)
    grad_extended, grad_taps = conv_pull(grad_conv_out)
    route = [(i + 1, i) for i in range(groups - 1)]
    sent_back = lax.ppermute(grad_extended[: KER - 1].astype(bf16), PLANE, route).astype(f32)
    grad_own = grad_extended[KER - 1 :]
    grad_proj = jnp.concatenate(
        (grad_own[: tokens - (KER - 1)], grad_own[tokens - (KER - 1) :] + sent_back)
    ).astype(bf16)
    grad_proj_a = grad_proj[:, :, :slice_width].reshape(tokens, 3 * slice_width)
    grad_proj_b = grad_proj[:, :, slice_width:].reshape(tokens, 3 * slice_width)
    grad_normed = dot(grad_proj_a, proj_a, c_cols) + dot(grad_proj_b, proj_b, c_cols)
    grad_normed = scatter_y(split_tokens(grad_normed))
    _, norm1_pull = jax.vjp(rms_norm, x_own.astype(f32), g_attn)
    grad_x_norm, grad_g_attn = norm1_pull(grad_normed)
    input_grad = from_sequence((grad_resid + grad_x_norm).astype(bf16), head)

    def both(own, other):
        return (own.astype(f32) + swap(other).astype(f32)).astype(bf16)

    ff_sum = both(*ff_grads)
    ff_sum = ff_sum.reshape(3, groups, -1, ff_slice).transpose(1, 0, 2, 3)
    ff_sum = lax.psum_scatter(ff_sum, PLANE, scatter_dimension=0, tiled=True)[0]
    ff_sum = ff_sum.reshape(3, RING, -1, ff_slice).transpose(1, 0, 2, 3)
    ff_sum = exchange(ff_sum, "y").astype(f32)

    grad_o_a = dot(grad_attn, gated[:, :slice_width], c_toks).astype(bf16)
    grad_o_b = dot(grad_attn, gated[:, slice_width:], c_toks).astype(bf16)
    attn_grad = both(
        jnp.concatenate((dot(normed, grad_proj_a, c_toks).astype(bf16), grad_o_a), axis=1),
        jnp.concatenate((dot(normed, grad_proj_b, c_toks).astype(bf16), grad_o_b), axis=1),
    )
    attn_sum = lax.psum_scatter(attn_grad, PLANE, scatter_dimension=0, tiled=True)
    attn_sum = exchange(attn_sum.reshape(RING, -1, 4 * slice_width), "y").astype(f32)

    def columns(v):
        return v.transpose(1, 0, 2).reshape(v.shape[1], -1)

    def turned(v):
        return v.transpose(0, 2, 1).reshape(-1, v.shape[1])

    grads = [columns(attn_sum[..., j * slice_width : (j + 1) * slice_width]) for j in range(3)]
    grad_w_o = turned(attn_sum[..., 3 * slice_width :])
    grad_w_gate, grad_w_up = columns(ff_sum[:, 0]), columns(ff_sum[:, 1])
    grad_w_down = turned(ff_sum[:, 2])

    per_channel = jnp.concatenate(
        (
            grad_taps.transpose(1, 0, 2).reshape(3 * KER, -1),
            grad_gap.reshape(1, -1),
            grad_gain_o.reshape(1, -1),
        )
    )
    per_feature = jnp.stack((grad_g_attn, grad_g_ffn))
    half = width // 2
    own = lax.dynamic_slice_in_dim(per_feature, head * half, half, 1)
    other = lax.dynamic_slice_in_dim(per_feature, (1 - head) * half, half, 1)

    def spread(v, rest):
        return jnp.concatenate(
            (lax.dynamic_update_slice(jnp.zeros((v.shape[0], half), f32), v, (0, place * slice_width)), rest)
        )

    small_grad = spread(per_channel[:, :slice_width], own) + swap(spread(per_channel[:, slice_width:], other))
    rows = small_grad.shape[0]
    count = lax.axis_size(SEQ)
    part = jnp.sum(exchange(small_grad.reshape(count, -1, 128), SEQ).reshape(count, -1), axis=0)
    part = jnp.broadcast_to(part.reshape(1, -1, 128), (count, part.shape[0] // 128, 128))
    small_grad = exchange(part, SEQ).reshape(rows, half)
    return (
        output,
        input_grad,
        grads[0],
        grads[1],
        grads[2],
        small_grad[: 3 * KER].reshape(3, KER, half),
        small_grad[3 * KER],
        small_grad[3 * KER + 1],
        grad_w_o,
        small_grad[3 * KER + 2],
        small_grad[3 * KER + 3],
        grad_w_gate,
        grad_w_up,
        grad_w_down,
    )


def solution(mesh):
    fine = Mesh(mesh.devices.reshape(4, 4, RING, 2), ("x", "z", "y", "head"))
    tokens = P(None, SEQ, "head")
    rows = P(SEQ, "head")
    columns = P("head", SEQ)
    channels = P("head")
    taps = P(None, None, "head")
    return jax.shard_map(
        body,
        mesh=fine,
        in_specs=(
            tokens,
            rows,
            rows,
            rows,
            taps,
            channels,
            channels,
            columns,
            channels,
            channels,
            rows,
            rows,
            columns,
            tokens,
        ),
        out_specs=(
            tokens,
            tokens,
            rows,
            rows,
            rows,
            taps,
            channels,
            channels,
            columns,
            channels,
            channels,
            rows,
            rows,
            columns,
        ),
        check_vma=False,
    )
```

time: 4510 us -> 831 us (0.18)
  waiting for transfers between devices: 3760 us -> 289 us
  blocking collectives: 195 us -> 31.3 us
  other arithmetic: 237 us -> 160 us
  starting transfers between devices: 4.53 us -> 80.6 us
    reduce_scatter x8 -> x1, waiting for transfers between devices: 2620 us -> 0.01 us  [body(): lax.psum_scatter(attn_grad, PLANE, scatter_dimension=0, tiled=True)]
    all_gather x11 -> x3, waiting for transfers between devices: 895 us -> 33.9 us  [the longest x1 21.3 us: gather_rows(): return lax.all_gather(held, PLANE, axis=0, tiled=True)]
    psum x4 -> x0, waiting for transfers between devices: 235 us -> none  [the longest x1 126 us: body(): lax.psum((grad_conv_local, grad_gap, grad_gain_out, attn_gain_half, ffn_g...]
    all_gather x3 -> x0, blocking collectives: 195 us -> none  [the longest x1 191 us: prefix(): gathered = jax.tree.map(lambda a: lax.all_gather(a, axis), part)]
    add x65 -> x9, other arithmetic: 184 us -> 11.2 us  [the longest x1 4.06 us: short_conv(): result = result + kernel[offset] * extended[offset:offset + length]]
    all_to_all x0 -> x15, waiting for transfers between devices: none -> 172 us  [exchange(): return lax.all_to_all(block, axis, 0, 0, tiled=True)]
    all_to_all x0 -> x15, starting transfers between devices: none -> 72.7 us  [exchange(): return lax.all_to_all(block, axis, 0, 0, tiled=True)]
    unnamed x23 -> x6, waiting for transfers between devices: 7.28 us -> 64.8 us
  transfers between devices with their start and end apart: 25 -> 34, of which waited for: 23 -> 21; matrix products, arithmetic and copies ran while one was open for 3% -> 28% of each run, Pallas kernels for 0% -> 0%
where the time goes in v1:
time: 831 us; the launch traced here: 819 us
  waiting for transfers between devices  289 us (35%)
  other arithmetic  160 us (19%)
  matrix products  138 us (17%)
  local copies, waits for them, and re-layouts  105 us (13%)
  starting transfers between devices  80.6 us (10%)
  blocking collectives  31.3 us (4%)
  between operations  16.2 us (2%)
    all_to_all x15, waiting for transfers between devices, exchange(): return lax.all_to_all(block, axis, 0, 0, tiled=True)  172 us
    dot_general x30, matrix products, dot(): lax.dot_general(a, b, (contract, ((), ())), preferred_element_type=f32)  103 us
    all_to_all x15, starting transfers between devices, exchange(): return lax.all_to_all(block, axis, 0, 0, tiled=True)  72.7 us
    unnamed x6, waiting for transfers between devices  64.8 us
    dot_general x12, matrix products, ein(): return jnp.einsum(form, a, b, precision=highest)  34.7 us
    all_to_all x3, blocking collectives, exchange(): return lax.all_to_all(block, axis, 0, 0, tiled=True)  31.3 us
    unnamed x23, other arithmetic  30.2 us
    another operation x1, other arithmetic, body(): lax.cumsum(grad_cumulative, axis=2, reverse=True) + grad_last[:, :, None, :]  30.2 us
  transfers between devices with their start and end apart: 34, of which 21 were waited for; matrix products, arithmetic and copies ran while one was open for 28% of the time, Pallas kernels for 0%

profile of v1, /device:TPU:0, one launch (start us, length us, event | category | flops | bytes accessed | tf_op | source)
XLA Modules:
  0.0 819.5 jit_solution(10471564628368829164)
XLA Ops:
  10.1 10.8 %all_to_all.90 = bf16[4,32,768]{2,1,0:T(8,128)(2,1)} all-to-all(bf16[4,32,768]{2,1,0:T(8,128)(2,1)S(1)} %copy.502), channel_id=1, replica_groups=mesh['x'=4,'z'=4,'y'=4,'head'=2] {'y'}, dimensions={0} | all-to-all | bytes 393216 | tf_op jit(solution)/shard_map/all_to_all | solution.py:25
  21.8 9.7 %all_to_all.91 = bf16[4,32,1024]{2,1,0:T(8,128)(2,1)} all-to-all(bf16[4,32,1024]{2,1,0:T(8,128)(2,1)S(1)} %broadcast_in_dim.94), channel_id=1, replica_groups=mesh['x'=4,'z'=4,'y'=4,'head'=2] {'y'}, dimensions={0} | all-to-all | bytes 524288 | tf_op jit(solution)/shard_map/all_to_all | solution.py:25
  34.0 10.8 %all_to_all.92 = bf16[4,3,32,704]{3,2,1,0:T(8,128)(2,1)S(1)} all-to-all(bf16[4,3,32,704]{3,2,1,0:T(8,128)(2,1)S(1)} %copy.538), channel_id=1, replica_groups=mesh['x'=4,'z'=4,'y'=4,'head'=2] {'y'}, dimensions={0} | all-to-all | bytes 1081344 | tf_op jit(solution)/shard_map/all_to_all | solution.py:25
  48.2 21.3 %all-gather.4.cloned.1.call-done = bf16[2048,768]{1,0:T(8,128)(2,1)} async-done(((bf16[128,768]{1,0:T(8,128)(2,1)}), bf16[2048,768]{1,0:T(8,128)(2,1)}) %all-gather.4.cloned.1.call-update) | async-done | bytes 3145744 | tf_op jit(solution)/shard_map/all_gather | solution.py:108
  76.8 25.6 %all-to-all-done = bf16[4,128,2048]{2,1,0:T(8,128)(2,1)S(1)} async-done(((bf16[4,128,2048]{2,1,0:T(8,128)(2,1)}), bf16[4,128,2048]{2,1,0:T(8,128)(2,1)S(1)}, u32[]{:S(2)}, u32[]{:S(2)}) %all-to-all-start) | async-done | bytes 2097184 | tf_op jit(solution)/shard_map/all_to_all | solution.py:25
  115.9 10.9 %collective-permute-done.4 = bf16[3,3,512]{0,2,1:T(8,128)(2,1)S(1)} collective-permute-done((bf16[3,3,512]{0,2,1:T(8,128)(2,1)S(1)}, bf16[3,3,512]{0,2,1:T(8,128)(2,1)S(1)}, u32[]{:S(2)}, u32[]{:S(2)}) %collective-permute-start.4) | collective-permute-done | bytes 9248 | tf_op jit(solution)/shard_map/ppermute | solution.py:191
  153.8 8.0 all-to-all-start.2
  165.9 8.5 %all-to-all-done.2 = f32[16,4,16,128]{3,2,1,0:T(8,128)} async-done(((f32[16,4,16,128]{3,2,1,0:T(8,128)}), f32[16,4,16,128]{3,2,1,0:T(8,128)}, u32[]{:S(2)}, u32[]{:S(2)}) %all-to-all-start.2) | async-done | bytes 524320 | tf_op jit(solution)/shard_map/all_to_all | solution.py:25
  200.2 12.6 %all-gather.8.cloned.1.call-done = bf16[3,2048,704]{2,1,0:T(8,128)(2,1)} async-done(((bf16[3,128,704]{2,1,0:T(8,128)(2,1)}), bf16[3,2048,704]{2,1,0:T(8,128)(2,1)}) %all-gather.8.cloned.1.call-update) | async-done | bytes 8650768 | tf_op jit(solution)/shard_map/all_gather | solution.py:149
  212.7 11.8 %copy.540 = bf16[3,2048,704]{1,2,0:T(8,128)(2,1)} copy(bf16[3,2048,704]{2,1,0:T(8,128)(2,1)} %all-gather.8.cloned.1.call-done) | data formatting | bytes 17301504 | tf_op jit(solution)/shard_map/all_gather | solution.py:149
  254.1 22.0 %all-to-all-done.4 = bf16[4,512,512]{1,2,0:T(8,128)(2,1)} async-done(((bf16[4,512,512]{1,2,0:T(8,128)(2,1)}), bf16[4,512,512]{1,2,0:T(8,128)(2,1)}, u32[]{:S(2)}, u32[]{:S(2)}) %all-to-all-start.4) | async-done | bytes 2097184 | tf_op jit(solution)/shard_map/all_to_all | solution.py:25
  302.0 7.8 all-to-all-done.8
  360.9 16.5 %all-to-all-done.9 = bf16[4,128,2048]{2,1,0:T(8,128)(2,1)} async-done(((bf16[4,128,2048]{2,1,0:T(8,128)(2,1)}), bf16[4,128,2048]{2,1,0:T(8,128)(2,1)}, u32[]{:S(2)}, u32[]{:S(2)}) %all-to-all-start.9) | async-done | bytes 2097184 | tf_op jit(solution)/shard_map/all_to_all | solution.py:25
  388.9 17.7 %all-to-all-done.7 = bf16[4,128,2048]{2,1,0:T(8,128)(2,1)} async-done(((bf16[4,128,2048]{2,1,0:T(8,128)(2,1)}), bf16[4,128,2048]{2,1,0:T(8,128)(2,1)}, u32[]{:S(2)}, u32[]{:S(2)}) %all-to-all-start.7) | async-done | bytes 2097184 | tf_op jit(solution)/shard_map/all_to_all | solution.py:25
  421.9 19.7 %all-to-all-done.10 = bf16[4,128,2048]{2,1,0:T(8,128)(2,1)} async-done(((bf16[4,128,2048]{2,1,0:T(8,128)(2,1)}), bf16[4,128,2048]{2,1,0:T(8,128)(2,1)}, u32[]{:S(2)}, u32[]{:S(2)}) %all-to-all-start.10) | async-done | bytes 2097184 | tf_op jit(solution)/shard_map/all_to_all | solution.py:25
  516.5 30.2 %reduce_window_sum.27 = f32[4,4,128,128]{3,2,1,0:T(8,128)} reduce-window(f32[4,4,128,128]{3,2,1,0:T(8,128)} %copy.568, f32[]{:T(128)} %constant.64.clone.1), window={size=1x1x128x1 pad=0_0x0_0x0_127x0_0}, to_apply=%region_10.11 | reduce-window | flops 33292288 | bytes 2097156 | tf_op jit(solution)/shard_map/body/reduce_window_sum | solution.py:306
  574.8 7.1 multiply_reduce_fusion.4
  581.9 7.2 fusion.132
  635.9 8.2 %bitcast_bitcast_fusion = bf16[16,3,128,704]{2,3,1,0:T(8,128)(2,1)} fusion(bf16[3,2048,704]{1,2,0:T(8,128)(2,1)} %collective-permute-done.13, bf16[1,2048,704]{1,2,0:T(8,128)(2,1)S(1)} %fusion.8, bf16[1,2048,704]{1,2,0:T(8,128)(2,1)S(1)} %fusion.7, bf16[1,2048,704]{1,2,0:T(8,128)(2,1)S(1)} %fusion.6), kind=kLoop, calls=%fused_computation.2 | loop fusion | flops 25952256 | bytes 25952256 | tf_op jit(solution)/shard_map/transpose | solution.py:332
  664.9 22.5 %all-to-all-done.13 = bf16[4,128,2048]{2,1,0:T(8,128)(2,1)} async-done(((bf16[4,128,2048]{2,1,0:T(8,128)(2,1)}), bf16[4,128,2048]{2,1,0:T(8,128)(2,1)}, u32[]{:S(2)}, u32[]{:S(2)}) %all-to-all-start.13) | async-done | bytes 2097184 | tf_op jit(solution)/shard_map/all_to_all | solution.py:25
  692.1 6.7 all-to-all-start.15
  699.0 9.5 %all-to-all-done.15 = f32[64,2,128]{2,1,0:T(2,128)S(1)} async-done(((f32[64,2,128]{2,1,0:T(2,128)}), f32[64,2,128]{2,1,0:T(2,128)S(1)}, u32[]{:S(2)}, u32[]{:S(2)}) %all-to-all-start.15) | async-done | bytes 65568 | tf_op jit(solution)/shard_map/all_to_all | solution.py:25
  715.0 8.7 %all-to-all-done.16 = f32[64,2,128]{2,1,0:T(2,128)S(1)} async-done(((f32[64,2,128]{2,1,0:T(2,128)}), f32[64,2,128]{2,1,0:T(2,128)S(1)}, u32[]{:S(2)}, u32[]{:S(2)}) %all-to-all-start.16) | async-done | bytes 65568 | tf_op jit(solution)/shard_map/all_to_all | solution.py:25
  728.4 64.7 %reduce-scatter.9.cloned.1.call-done = bf16[1,3,128,704]{2,3,1,0:T(8,128)(2,1)} async-done(((bf16[16,3,128,704]{2,3,1,0:T(8,128)(2,1)}), bf16[1,3,128,704]{2,3,1,0:T(8,128)(2,1)}) %reduce-scatter.9.cloned.1.call-update) | async-done | bytes 540688
  (534 shorter events, 424.8 us)
Async XLA Ops:
  7.2 62.3 %all-gather.4.cloned.1.call-start = ((), (), s32[]{:S(2)}) async-start(), calls=%async_computation.20 | async-start | bytes 3342336 | tf_op jit(solution)/shard_map/all_gather | solution.py:108
  20.9 141.5 %all-gather.6.cloned.1.call-start = ((), (), s32[]{:S(2)}) async-start(), calls=%async_computation.21 | async-start | bytes 4456448 | tf_op jit(solution)/shard_map/all_gather | solution.py:144
  31.6 181.1 %all-gather.8.cloned.1.call-start = ((), (), s32[]{:S(2)}) async-start(), calls=%async_computation.22 | async-start | bytes 10027008 | tf_op jit(solution)/shard_map/all_gather | solution.py:149
  46.0 29.7 %collective-permute-start.2 = (bf16[2,1024]{1,0:T(2,128)(2,1)S(1)}, bf16[2,1024]{1,0:T(2,128)(2,1)S(1)}, u32[]{:S(2)}, u32[]{:S(2)}) collective-permute-start(bf16[2,1024]{1,0:T(2,128)(2,1)S(1)} %pad_maximum_fusion.22), channel_id=1, source_target_pairs={{0,1},{1,0},{2,3},{3,2},{4,5},{5,4},{6,7},{7,6},{8,9},{9,8},{10,11... | collective-permute-start | bytes 12296 | tf_op jit(solution)/shard_map/ppermute | solution.py:21
  69.5 37.9 %collective-permute-start.3 = (bf16[2048,768]{1,0:T(8,128)(2,1)}, bf16[2048,768]{1,0:T(8,128)(2,1)}, u32[]{:S(2)}, u32[]{:S(2)}) collective-permute-start(bf16[2048,768]{1,0:T(8,128)(2,1)} %all-gather.4.cloned.1.call-done), channel_id=1, source_target_pairs={{0,1},{1,0},{2,3},{3,2},{4,5},{5,4},{6,7},{7,6},{8,9},{9,8},{10,11... | collective-permute-start | bytes 9437192 | tf_op jit(solution)/shard_map/ppermute | solution.py:21
  71.1 31.3 %all-to-all-start = ((bf16[4,128,2048]{2,1,0:T(8,128)(2,1)}), bf16[4,128,2048]{2,1,0:T(8,128)(2,1)S(1)}, u32[]{:S(2)}, u32[]{:S(2)}) async-start(bf16[4,128,2048]{2,1,0:T(8,128)(2,1)} %broadcast_in_dim.40), calls=%async_computation | async-start | bytes 4194304 | tf_op jit(solution)/shard_map/all_to_all | solution.py:25
  153.8 20.5 %all-to-all-start.2 = ((f32[16,4,16,128]{3,2,1,0:T(8,128)}), f32[16,4,16,128]{3,2,1,0:T(8,128)}, u32[]{:S(2)}, u32[]{:S(2)}) async-start(f32[16,4,16,128]{3,2,1,0:T(8,128)} %fusion.78), calls=%async_computation.2 | async-start | bytes 1048576 | tf_op jit(solution)/shard_map/all_to_all | solution.py:25
  162.4 126.2 %collective-permute-start.5 = (bf16[2048,1024]{1,0:T(8,128)(2,1)}, bf16[2048,1024]{1,0:T(8,128)(2,1)}, u32[]{:S(2)}, u32[]{:S(2)}) collective-permute-start(bf16[2048,1024]{1,0:T(8,128)(2,1)} %all-gather.6.cloned.1.call-done), channel_id=1, source_target_pairs={{0,1},{1,0},{2,3},{3,2},{4,5},{5,4},{6,7},{7,6},{8,9},{9,8},{10,11... | collective-permute-start | bytes 12582920 | tf_op jit(solution)/shard_map/ppermute | solution.py:21
  194.8 33.0 %all-to-all-start.3 = ((f32[16,4,8,128]{3,2,1,0:T(8,128)}), f32[16,4,8,128]{3,2,1,0:T(8,128)S(1)}, u32[]{:S(2)}, u32[]{:S(2)}) async-start(f32[16,4,8,128]{3,2,1,0:T(8,128)} %constant_dynamic-update-slice_fusion), calls=%async_computation.3 | async-start | bytes 524288 | tf_op jit(solution)/shard_map/all_to_all | solution.py:25
  224.5 100.3 %collective-permute-start.6 = (bf16[3,2048,704]{1,2,0:T(8,128)(2,1)}, bf16[3,2048,704]{1,2,0:T(8,128)(2,1)}, u32[]{:S(2)}, u32[]{:S(2)}) collective-permute-start(bf16[3,2048,704]{1,2,0:T(8,128)(2,1)} %copy.540), channel_id=1, source_target_pairs={{0,1},{1,0},{2,3},{3,2},{4,5},{5,4},{6,7},{7,6},{8,9},{9,8},{10,11... | collective-permute-start | bytes 25952264 | tf_op jit(solution)/shard_map/ppermute | solution.py:21
  244.3 31.8 %all-to-all-start.4 = ((bf16[4,512,512]{1,2,0:T(8,128)(2,1)}), bf16[4,512,512]{1,2,0:T(8,128)(2,1)}, u32[]{:S(2)}, u32[]{:S(2)}) async-start(bf16[4,512,512]{1,2,0:T(8,128)(2,1)} %broadcast_in_dim.48), calls=%async_computation.4 | async-start | bytes 4194304 | tf_op jit(solution)/shard_map/all_to_all | solution.py:25
  278.8 31.0 %all-to-all-start.8 = ((bf16[4,128,2048]{2,1,0:T(8,128)(2,1)}), bf16[4,128,2048]{2,1,0:T(8,128)(2,1)}, u32[]{:S(2)}, u32[]{:S(2)}) async-start(bf16[4,128,2048]{2,1,0:T(8,128)(2,1)} %broadcast_in_dim.95), calls=%async_computation.8 | async-start | bytes 4194304 | tf_op jit(solution)/shard_map/all_to_all | solution.py:25
  347.3 30.1 %all-to-all-start.9 = ((bf16[4,128,2048]{2,1,0:T(8,128)(2,1)}), bf16[4,128,2048]{2,1,0:T(8,128)(2,1)}, u32[]{:S(2)}, u32[]{:S(2)}) async-start(bf16[4,128,2048]{2,1,0:T(8,128)(2,1)} %bitcast.423), calls=%async_computation.9 | async-start | bytes 4194304 | tf_op jit(solution)/shard_map/all_to_all | solution.py:25
  377.4 29.2 %all-to-all-start.7 = ((bf16[4,128,2048]{2,1,0:T(8,128)(2,1)}), bf16[4,128,2048]{2,1,0:T(8,128)(2,1)}, u32[]{:S(2)}, u32[]{:S(2)}) async-start(bf16[4,128,2048]{2,1,0:T(8,128)(2,1)} %bitcast.432), calls=%async_computation.7 | async-start | bytes 4194304 | tf_op jit(solution)/shard_map/all_to_all | solution.py:25
  413.2 28.4 %all-to-all-start.10 = ((bf16[4,128,2048]{2,1,0:T(8,128)(2,1)}), bf16[4,128,2048]{2,1,0:T(8,128)(2,1)}, u32[]{:S(2)}, u32[]{:S(2)}) async-start(bf16[4,128,2048]{2,1,0:T(8,128)(2,1)} %broadcast_in_dim.97), calls=%async_computation.10 | async-start | bytes 4194304 | tf_op jit(solution)/shard_map/all_to_all | solution.py:25
  496.7 227.7 %reduce-scatter.7.cloned.1.call-start = ((), (), s32[]{:S(2)}) async-start(), calls=%async_computation.23 | async-start | bytes 4456448 | tf_op jit(solution)/shard_map/reduce_scatter | solution.py:343
  602.8 15.6 %collective-permute-start.11 = (bf16[2048,1024]{0,1:T(8,128)(2,1)S(1)}, bf16[2048,1024]{0,1:T(8,128)(2,1)S(1)}, u32[]{:S(2)}, u32[]{:S(2)}) collective-permute-start(bf16[2048,1024]{0,1:T(8,128)(2,1)S(1)} %pad_maximum_fusion.1), channel_id=1, source_target_pairs={{0,1},{1,0},{2,3},{3,2},{4,5},{5,4},{6,7},{7,6},{8,9},{9,8},{10,11... | collective-permute-start | bytes 12582920 | tf_op jit(solution)/shard_map/ppermute | solution.py:21
  614.3 21.6 %collective-permute-start.13 = (bf16[3,2048,704]{1,2,0:T(8,128)(2,1)}, bf16[3,2048,704]{1,2,0:T(8,128)(2,1)}, u32[]{:S(2)}, u32[]{:S(2)}) collective-permute-start(bf16[3,2048,704]{1,2,0:T(8,128)(2,1)} %pad_maximum_fusion), channel_id=1, source_target_pairs={{0,1},{1,0},{2,3},{3,2},{4,5},{5,4},{6,7},{7,6},{8,9},{9,8},{10,11... | collective-permute-start | bytes 25952264 | tf_op jit(solution)/shard_map/ppermute | solution.py:21
  628.4 164.7 %reduce-scatter.9.cloned.1.call-start = ((), (), s32[]{:S(2)}) async-start(), calls=%async_computation.24 | async-start | bytes 9191424
  655.8 31.6 %all-to-all-start.13 = ((bf16[4,128,2048]{2,1,0:T(8,128)(2,1)}), bf16[4,128,2048]{2,1,0:T(8,128)(2,1)}, u32[]{:S(2)}, u32[]{:S(2)}) async-start(bf16[4,128,2048]{2,1,0:T(8,128)(2,1)} %bitcast.431), calls=%async_computation.13 | async-start | bytes 4194304 | tf_op jit(solution)/shard_map/all_to_all | solution.py:25
  692.1 16.3 %all-to-all-start.15 = ((f32[64,2,128]{2,1,0:T(2,128)}), f32[64,2,128]{2,1,0:T(2,128)S(1)}, u32[]{:S(2)}, u32[]{:S(2)}) async-start(f32[64,2,128]{2,1,0:T(2,128)} %reshape.405), calls=%async_computation.15 | async-start | bytes 131072 | tf_op jit(solution)/shard_map/all_to_all | solution.py:25
  698.9 100.7 %collective-permute-start.10 = (bf16[128,1024]{1,0:T(8,128)(2,1)S(1)}, bf16[128,1024]{1,0:T(8,128)(2,1)S(1)}, u32[]{:S(2)}, u32[]{:S(2)}) collective-permute-start(bf16[128,1024]{1,0:T(8,128)(2,1)S(1)} %constant_dynamic-slice_fusion), channel_id=1, source_target_pairs={{0,1},{1,0},{2,3},{3,2},{4,5},{5,4},{6,7},{7,6},{8,9},{9,8},{10,11... | collective-permute-start | bytes 786440 | tf_op jit(solution)/shard_map/ppermute | solution.py:21
  709.2 14.5 %all-to-all-start.16 = ((f32[64,2,128]{2,1,0:T(2,128)}), f32[64,2,128]{2,1,0:T(2,128)S(1)}, u32[]{:S(2)}, u32[]{:S(2)}) async-start(f32[64,2,128]{2,1,0:T(2,128)} %broadcast_in_dim.100), calls=%async_computation.16 | async-start | bytes 131072 | tf_op jit(solution)/shard_map/all_to_all | solution.py:25
  724.4 70.9 %all-to-all-start.14 = ((bf16[4,32,1024]{2,1,0:T(8,128)(2,1)}), bf16[4,32,1024]{2,1,0:T(8,128)(2,1)S(1)}, u32[]{:S(2)}, u32[]{:S(2)}) async-start(bf16[4,32,1024]{2,1,0:T(8,128)(2,1)} %bitcast.450), calls=%async_computation.14 | async-start | bytes 524288 | tf_op jit(solution)/shard_map/all_to_all | solution.py:25
  (121 other events, 1385.4 us)
Sparse Core Ops, SparseCore 0:
  21.0 48.4 all-gather.3
  71.6 50.7 all-gather.5
  124.6 88.0 all-gather.7
  628.5 75.8 reduce-scatter.6
  708.1 85.0 reduce-scatter.8
